TPU v7x, 32 devices: a whole 2x2x4 slice. The times are simulated.
32 devices in a mesh: fsdp: 16 (over z, x, core), tp: 2 (over y).
Axes of the slice: x: 2, y: 2, z: 4, core: 2. Of those that a mesh axis runs over, the one named last changes fastest.
Arguments:
- grad_kv: bfloat16 [16, 4096, 1024], P('fsdp', None, 'tp'), may hold values from -4 to 4
- grad_gains: bfloat16 [16, 2, 8192], P('fsdp', 'tp'), may hold values from -4 to 4
- kv_weight: float32 [4096, 1024], P('fsdp', 'tp'), may hold values from -0.125 to 0.125
- kv_first: float32 [4096, 1024], P('fsdp', 'tp'), may hold values from -2 to 2
- kv_second: float32 [4096, 1024], P('fsdp', 'tp'), may hold values from 0.004 to 0.4
- gain_weight: float32 [8192], P(('fsdp', 'tp')), may hold values from 0.5 to 1.5
- gain_first: float32 [8192], P(('fsdp', 'tp')), may hold values from -2 to 2
- gain_second: float32 [8192], P(('fsdp', 'tp')), may hold values from 0.05 to 5
- average: bfloat16 [16, 256, 1024], P(None, 'tp'), may hold values from -0.125 to 0.125
Outputs:
- kv_weight_out: float32 [4096, 1024], P('fsdp', 'tp')
- kv_first_out: float32 [4096, 1024], P('fsdp', 'tp')
- kv_second_out: float32 [4096, 1024], P('fsdp', 'tp')
- gain_weight_out: float32 [8192], P(('fsdp', 'tp'))
- gain_first_out: float32 [8192], P(('fsdp', 'tp'))
- gain_second_out: float32 [8192], P(('fsdp', 'tp'))
- kv_blocks: bfloat16 [4096, 1024], P(None, 'tp')
- gain_copy: bfloat16 [8192], replicated
- average_out: bfloat16 [16, 256, 1024], P(None, 'tp')
All inputs are finite; a program needn't handle non-finite values.
Results may differ from a plain program's by a relative error of at most 0.003.
Values may be sent and summed in bfloat16 or wider, within the bound.
A program may use at most 64 MiB of HBM per device.

v0:
```python
import jax
import jax.numpy as jnp
from jax import lax
from jax.sharding import PartitionSpec as P

STEP = 100
PARAMS = 4202496


def adam_update(grad, first, second, weight, factor, decay):
    clipped = factor * grad
    first_new = 0.9 * first + 0.1 * clipped
    second_new = 0.95 * second + 0.05 * clipped * clipped
    first_fix = 1.0 - 0.9**STEP
    second_fix = 1.0 - 0.95**STEP
    step_dir = first_new / first_fix / (jnp.sqrt(second_new / second_fix) + 1e-08)
    weight_new = weight - 0.001 * (step_dir + decay * weight)
    return (weight_new, first_new, second_new)


def shards(
    grad_kv,
    grad_gains,
    kv_weight,
    kv_first,
    kv_second,
    gain_weight,
    gain_first,
    gain_second,
    average,
):
    kv_piece = lax.psum_scatter(
        grad_kv[0].astype(jnp.float32), "fsdp", scatter_dimension=0, tiled=True
    )
    kv_square = jnp.sum(kv_piece * kv_piece)
    flat_gain = grad_gains.reshape(-1).astype(jnp.float32)
    gain_piece = lax.psum_scatter(flat_gain, ("fsdp", "tp"), scatter_dimension=0, tiled=True)
    total = lax.psum(kv_square + jnp.sum(gain_piece * gain_piece), ("fsdp", "tp"))
    factor = jnp.minimum(jnp.float32(1.0), 1.0 / jnp.sqrt(total / PARAMS + 1e-06))
    kv_w, kv_m, kv_v = adam_update(kv_piece, kv_first, kv_second, kv_weight, factor, 0.1)
    gain_w, gain_m, gain_v = adam_update(
        gain_piece, gain_first, gain_second, gain_weight, factor, 0.0
    )
    gain_copy = lax.all_gather(gain_w.astype(jnp.bfloat16), ("fsdp", "tp"), axis=0, tiled=True)
    kv_rounded = kv_w.astype(jnp.bfloat16)
    kv_blocks = lax.all_gather(kv_rounded, "fsdp", axis=0, tiled=True)
    shard_count = lax.axis_size("fsdp")
    tp_count = lax.axis_size("tp")
    columns = kv_rounded.shape[1]
    row_count = kv_rounded.shape[0] // tp_count
    moved = lax.all_to_all(
        kv_blocks.reshape(shard_count, tp_count, row_count, columns),
        "tp",
        split_axis=1,
        concat_axis=3,
        tiled=True,
    )
    moved = moved.reshape(shard_count, row_count, columns * tp_count)
    blended = 0.8 * average.astype(jnp.float32) + 0.2 * moved.astype(jnp.float32)
    average_out = blended.astype(jnp.bfloat16)
    return (kv_w, kv_m, kv_v, gain_w, gain_m, gain_v, kv_blocks, gain_copy, average_out)


def solution(mesh):
    in_specs = (
        P("fsdp", None, "tp"),
        P("fsdp", "tp", None),
        P("fsdp", "tp"),
        P("fsdp", "tp"),
        P("fsdp", "tp"),
        P(("fsdp", "tp")),
        P(("fsdp", "tp")),
        P(("fsdp", "tp")),
        P(None, "tp", None),
    )
    out_specs = (
        P("fsdp", "tp"),
        P("fsdp", "tp"),
        P("fsdp", "tp"),
        P(("fsdp", "tp")),
        P(("fsdp", "tp")),
        P(("fsdp", "tp")),
        P(None, "tp"),
        P(),
        P(None, "tp", None),
    )
    return jax.shard_map(shards, mesh=mesh, in_specs=in_specs, out_specs=out_specs, check_vma=False)
```

profile of v0, /device:TPU:1, one launch (start us, length us, event | category | flops | bytes accessed | tf_op | source)
XLA Modules:
  0.0 362.4 jit_solution(8025539764088087996)
XLA Ops:
  7.2 0.0 reduce-scatter.2.cloned.1.call-start
  7.2 6.6 %bitcast_convert_fusion = f32[4096,512]{1,0:T(8,128)} fusion(bf16[1,4096,512]{2,1,0:T(8,128)(2,1)} %param.9), kind=kLoop, calls=%fused_computation.3 | loop fusion | flops 2097152 | bytes 12582912 | tf_op jit(solution)/shard_map/convert_element_type | solution.py:33
  13.8 0.0 reduce-scatter.2.cloned.1.call-update
  13.9 0.0 all-gather.3.cloned.1.call-start
  13.9 0.7 copy-done.4
  14.6 41.7 %all-reduce = f32[8192]{0:T(1024)S(1)} all-reduce(f32[8192]{0:T(1024)S(1)} %bitcast.16), channel_id=3, replica_groups=mesh['fsdp'=16,'tp'=2] {'fsdp','tp'}, use_global_device_ids=true, to_apply=%region_2.0.clone | all-reduce | flops 8192 | bytes 65536
  56.3 0.7 multiply_reduce_fusion.1
  57.0 63.9 %reduce-scatter.2.cloned.1.call-done = f32[256,512]{1,0:T(8,128)} async-done(((f32[4096,512]{1,0:T(8,128)}), f32[256,512]{1,0:T(8,128)}) %reduce-scatter.2.cloned.1.call-update) | async-done | bytes 524304 | tf_op jit(solution)/shard_map/reduce_scatter | solution.py:32
  120.8 1.8 multiply_reduce_fusion
  123.9 39.7 %psum.7 = f32[]{:T(128)} all-reduce(f32[]{:T(128)S(6)} %add.45), channel_id=1, replica_groups=mesh['fsdp'=16,'tp'=2] {'fsdp','tp'}, use_global_device_ids=true, to_apply=%region_4.0 | all-reduce | flops 1 | bytes 8 | tf_op jit(solution)/shard_map/psum | solution.py:38
  164.3 0.0 copy-done.1
  164.3 2.6 fusion.5
  166.9 0.0 all-gather.3.cloned.1.call-update
  166.9 51.4 %all-gather.3.cloned.1.call-done = bf16[4096,512]{1,0:T(8,128)(2,1)} async-done(((bf16[256,512]{1,0:T(8,128)(2,1)}), bf16[4096,512]{1,0:T(8,128)(2,1)}) %all-gather.3.cloned.1.call-update) | async-done | bytes 4194320 | tf_op jit(solution)/shard_map/all_gather | solution.py:46
  218.3 4.6 %copy.21 = bf16[16,2,128,512]{3,2,0,1:T(8,128)(2,1)} copy(bf16[16,2,128,512]{3,2,1,0:T(8,128)(2,1)} %bitcast.15) | data formatting | bytes 8388608 | tf_op jit(solution)/shard_map/reshape | solution.py:52
  223.0 5.6 %all-to-all-start = ((bf16[16,2,128,512]{3,2,0,1:T(8,128)(2,1)}), bf16[16,2,128,512]{3,2,0,1:T(8,128)(2,1)}, u32[]{:S(2)}, u32[]{:S(2)}) async-start(bf16[16,2,128,512]{3,2,0,1:T(8,128)(2,1)} %copy.21), calls=%async_computation.1 | async-start | bytes 8388608 | tf_op jit(solution)/shard_map/all_to_all | solution.py:51
  228.6 0.0 copy-start.5
  228.6 0.0 copy-start.6
  228.6 0.0 copy-start.7
  228.6 6.4 %copy.20 = bf16[16,128,1024]{1,2,0:T(8,128)(2,1)} copy(bf16[16,128,1024]{2,1,0:T(8,128)(2,1)} %param.17) | data formatting | bytes 8388608 | tf_op args[8]
  235.0 0.0 copy-done.6
  235.0 0.7 fusion.3
  235.7 95.2 %all-gather = bf16[32,1,256]{2,1,0:T(2,128)(2,1)S(1)} all-gather(bf16[1,1,256]{2,1,0:T(2,128)(2,1)S(1)} %reshape.37), channel_id=1, replica_groups=mesh['fsdp'=16,'tp'=2] {'fsdp','tp'}, dimensions={0}, use_global_device_ids=true | all-gather | bytes 16896 | tf_op jit(solution)/shard_map/all_gather | solution.py:44
  330.9 0.1 reduce
  331.0 0.6 copy.24
  331.6 0.0 all-to-all-done
  331.6 6.4 %copy.22 = bf16[16,2,128,512]{2,3,1,0:T(8,128)(2,1)} copy(bf16[16,2,128,512]{3,2,0,1:T(8,128)(2,1)} %all-to-all-done) | data formatting | bytes 8388608 | tf_op jit(solution)/shard_map/all_to_all | solution.py:51
  338.0 3.4 convert_multiply_fusion
  341.3 0.1 copy-done
  341.4 3.2 fusion
  344.7 6.4 %copy.23 = bf16[16,128,1024]{2,1,0:T(8,128)(2,1)} copy(bf16[16,128,1024]{1,2,0:T(8,128)(2,1)} %fusion) | data formatting | bytes 8388608
  351.0 4.5 %copy.26 = bf16[4096,512]{1,0:T(8,128)(2,1)} copy(bf16[4096,512]{1,0:T(8,128)(2,1)} %all-gather.3.cloned.1.call-done) | data formatting | bytes 8388608
  (11 shorter events, 0.1 us)
Async XLA Ops:
  7.2 113.7 %reduce-scatter.2.cloned.1.call-start = ((), (), s32[]{:S(2)}) async-start(), calls=%async_computation.2 | async-start | bytes 8912896 | tf_op jit(solution)/shard_map/reduce_scatter | solution.py:32
  13.8 0.8 copy-start.4
  13.8 150.5 %copy-start.1 = (f32[256,512]{1,0:T(8,128)S(1)}, f32[256,512]{1,0:T(8,128)}, u32[]{:S(2)}) copy-start(f32[256,512]{1,0:T(8,128)} %param.11) | copy-start | bytes 1572868
  13.8 150.5 %copy-start.2 = (f32[256,512]{1,0:T(8,128)S(1)}, f32[256,512]{1,0:T(8,128)}, u32[]{:S(2)}) copy-start(f32[256,512]{1,0:T(8,128)} %param.12) | copy-start | bytes 1572868
  13.8 150.5 %copy-start.3 = (f32[256,512]{1,0:T(8,128)S(1)}, f32[256,512]{1,0:T(8,128)}, u32[]{:S(2)}) copy-start(f32[256,512]{1,0:T(8,128)} %param.13) | copy-start | bytes 1572868
  13.9 204.5 %all-gather.3.cloned.1.call-start = ((), (), s32[]{:S(2)}) async-start(), calls=%async_computation.3 | async-start | bytes 4456448 | tf_op jit(solution)/shard_map/all_gather | solution.py:46
  223.0 108.6 %all-to-all-start = ((bf16[16,2,128,512]{3,2,0,1:T(8,128)(2,1)}), bf16[16,2,128,512]{3,2,0,1:T(8,128)(2,1)}, u32[]{:S(2)}, u32[]{:S(2)}) async-start(bf16[16,2,128,512]{3,2,0,1:T(8,128)(2,1)} %copy.21), calls=%async_computation.1 | async-start | bytes 8388608 | tf_op jit(solution)/shard_map/all_to_all | solution.py:51
  228.6 6.4 %copy-start.5 = (f32[256]{0:T(256)S(1)}, f32[256]{0:T(256)}, u32[]{:S(2)}) copy-start(f32[256]{0:T(256)} %param.14) | copy-start | bytes 3076
  228.6 6.4 %copy-start.6 = (f32[256]{0:T(256)S(1)}, f32[256]{0:T(256)}, u32[]{:S(2)}) copy-start(f32[256]{0:T(256)} %param.15) | copy-start | bytes 3076
  228.6 6.4 %copy-start.7 = (f32[256]{0:T(256)S(1)}, f32[256]{0:T(256)}, u32[]{:S(2)}) copy-start(f32[256]{0:T(256)} %param.16) | copy-start | bytes 3076
  338.0 3.4 copy-start
Sparse Core Ops, SparseCore 0:
  14.0 106.8 reduce-scatter.1
  167.0 51.2 all-gather.2
where the time goes:
time: 366 us; the launch traced here: 362 us
  blocking collectives  177 us (48%)
  waiting for transfers between devices  115 us (31%)
  local copies, waits for them, and re-layouts  29.7 us (8%)
  other arithmetic  19 us (5%)
  between operations  16.1 us (4%)
  starting transfers between devices  5.67 us (2%)
    all_gather x1, blocking collectives, shards(): lax.all_gather(gain_w.astype(jnp.bfloat16), ('fsdp', 'tp'), axis=0, tiled...  95.2 us
    reduce_scatter x1, waiting for transfers between devices, shards(): lax.psum_scatter(grad_kv[0].astype(jnp.float32), 'fsdp', scatter_dimensio...  63.9 us
    all_gather x1, waiting for transfers between devices, shards(): kv_blocks = lax.all_gather(kv_rounded, 'fsdp', axis=0, tiled=True)  51.4 us
    unnamed x1, blocking collectives  41.7 us
    psum x1, blocking collectives, shards(): lax.psum(kv_square + jnp.sum(gain_piece * gain_piece), ('fsdp', 'tp'))  39.7 us
    unnamed x21, local copies, waits for them, and re-layouts  18.7 us
  transfers between devices with their start and end apart: 3, of which 2 were waited for; matrix products, arithmetic and copies ran while one was open for 2% of the time, Pallas kernels for 0%

commit v1 on v0

--- a/solution.py
+++ b/solution.py
@@ -1,10 +1,15 @@
+import functools
+
 import jax
 import jax.numpy as jnp
 from jax import lax
+from jax.experimental import pallas as pl
+from jax.experimental.pallas import tpu as pltpu
 from jax.sharding import PartitionSpec as P
 
 STEP = 100
 PARAMS = 4202496
+TILE = 32
 
 
 def adam_update(grad, first, second, weight, factor, decay):
@@ -16,6 +21,511 @@
     step_dir = first_new / first_fix / (jnp.sqrt(second_new / second_fix) + 1e-08)
     weight_new = weight - 0.001 * (step_dir + decay * weight)
     return (weight_new, first_new, second_new)
+
+
+def step_kernel(
+    depth,
+    grad,
+    gain_grad,
+    w_in,
+    m_in,
+    v_in,
+    gw_in,
+    gm_in,
+    gv_in,
+    avg_in,
+    w_out,
+    m_out,
+    v_out,
+    gw_out,
+    gm_out,
+    gv_out,
+    kv_out,
+    copy_out,
+    avg_out,
+    own,
+    land1,
+    send2,
+    land2,
+    send3,
+    land3,
+    acc,
+    wbuf,
+    mbuf,
+    vbuf,
+    avg,
+    kv,
+    other,
+    gsum,
+    gland,
+    gz,
+    states,
+    t1,
+    t2,
+    own_sem,
+    load_sem,
+    store_sem,
+    p1s,
+    p1r,
+    p2s,
+    p2r,
+    p3s,
+    p3r,
+    gs,
+    gr,
+    ss,
+    sr,
+    t1s,
+    t1r,
+    t2s,
+    t2r,
+    azs,
+    azr,
+    axs,
+    axr,
+    acs,
+    acr,
+    ays,
+    ayr,
+    aos,
+    aor,
+    kvo_sem,
+    avo_sem,
+):
+    f32, bf16 = jnp.float32, jnp.bfloat16
+    f = lax.axis_index("fsdp")
+    t = lax.axis_index("tp")
+    c = lax.rem(f, 2)
+    x = lax.rem(lax.div(f, 2), 2)
+    z = lax.div(f, 4)
+    rows, cols = acc.shape
+    half = rows // 2
+
+    def index(zz, xx, cc):
+        return (zz * 2 + xx) * 2 + cc
+
+    def flip(bit, by):
+        return 1 - bit if by else bit
+
+    def ahead(s):
+        return lax.rem(z + s, depth)
+
+    def behind(s):
+        return lax.rem(z + depth - s, depth)
+
+    core_peer = (index(z, x, 1 - c), t)
+    x_peer = (index(z, 1 - x, c), t)
+    y_peer = (f, 1 - t)
+
+    def z_peer(s):
+        return (index(ahead(s), x, c), t)
+
+    def near_peer(k):
+        return (index(z, flip(x, k // 4), flip(c, (k // 2) % 2)), flip(t, k % 2))
+
+    pending = []
+
+    def push(src, dst, ssem, rsem, to):
+        copy = pltpu.make_async_remote_copy(
+            src_ref=src,
+            dst_ref=dst,
+            send_sem=ssem,
+            recv_sem=rsem,
+            device_id=to,
+            device_id_type=pl.DeviceIdType.MESH,
+        )
+        copy.start()
+        pending.append(copy.wait_send)
+        return copy
+
+    def local(src, dst, sem):
+        copy = pltpu.make_async_copy(src, dst, sem)
+        copy.start()
+        return copy
+
+    barrier = pltpu.get_barrier_semaphore()
+    partners = [near_peer(k) for k in range(1, 8)] + [z_peer(s) for s in range(1, depth)]
+    for to in partners:
+        pl.semaphore_signal(barrier, inc=1, device_id=to, device_id_type=pl.DeviceIdType.MESH)
+
+    order = [depth // 2] + [s for s in range(1, depth) if s != depth // 2] + [0]
+    own_copy, hop1, hop2, hop3 = {}, {}, {}, {}
+    for s in order:
+        for dx in (1, 0):
+            j = s * 2 + dx
+            own_copy[j] = local(grad.at[index(ahead(s), flip(x, dx), c)], own.at[j], own_sem.at[j])
+    pl.semaphore_wait(barrier, len(partners))
+
+    def piece(h):
+        return pl.ds(h * half, half)
+
+    for s in order:
+        for dx in (1, 0):
+            j = s * 2 + dx
+            for h in range(2):
+                hop1[j, h] = push(
+                    grad.at[index(ahead(s), flip(x, dx), 1 - c), piece(h)],
+                    land1.at[j, piece(h)],
+                    p1s.at[j, h],
+                    p1r.at[j, h],
+                    core_peer,
+                )
+    loads = [
+        local(w_in, wbuf, load_sem.at[0]),
+        local(m_in, mbuf, load_sem.at[1]),
+        local(v_in, vbuf, load_sem.at[2]),
+        local(avg_in, avg, load_sem.at[3]),
+    ]
+
+    place = f * 2 + t
+    gsum[0] = gain_grad[...].astype(f32)
+    states[place] = jnp.zeros(states.shape[1:], f32)
+    states[place, 0:1, :] = gw_in[...]
+    states[place, 1:2, :] = gm_in[...]
+    states[place, 2:3, :] = gv_in[...]
+    near = [y_peer, core_peer, x_peer]
+    gain_hop, state_hop = {}, {}
+
+    def gain_send(stage):
+        count = 1 << stage
+        span = pl.ds(place - lax.rem(place, count), count)
+        if stage < 3:
+            gain_hop[stage] = push(
+                gsum.at[stage], gland.at[stage], gs.at[stage], gr.at[stage], near[stage]
+            )
+            state_hop[stage] = push(
+                states.at[span], states.at[span], ss.at[stage], sr.at[stage], near[stage]
+            )
+        else:
+            for s in range(1, depth):
+                k = 2 + s
+                gain_hop[k] = push(gz.at[z], gz.at[z], gs.at[k], gr.at[k], z_peer(s))
+                state_hop[k] = push(states.at[span], states.at[span], ss.at[k], sr.at[k], z_peer(s))
+
+    def gain_take(stage):
+        gain_hop[stage].wait_recv()
+        state_hop[stage].wait_recv()
+        total = gsum[stage] + gland[stage]
+        if stage < 2:
+            gsum[stage + 1] = total
+        else:
+            gz[z] = total
+
+    gain_send(0)
+
+    def tiles(base, count, body, init=None):
+        def step(i, carry):
+            return body(pl.ds(pl.multiple_of(base + i * TILE, TILE), TILE), carry)
+
+        return lax.fori_loop(0, count // TILE, step, init)
+
+    for at, s in enumerate(order):
+        j = s * 2 + 1
+        own_copy[j].wait()
+        for h in range(2):
+            hop1[j, h].wait_recv()
+
+            def add2(r, carry, j=j, s=s):
+                send2[s, r] = (own[j, r].astype(f32) + land1[j, r].astype(f32)).astype(bf16)
+                return carry
+
+            tiles(h * half, half, add2, 0)
+            hop2[s, h] = push(
+                send2.at[s, piece(h)], land2.at[s, piece(h)], p2s.at[s, h], p2r.at[s, h], x_peer
+            )
+
+    for at, s in enumerate(order):
+        j = s * 2
+        own_copy[j].wait()
+        for h in range(2):
+            hop1[j, h].wait_recv()
+            hop2[s, h].wait_recv()
+
+            def add3(r, carry, j=j, s=s):
+                value = own[j, r].astype(f32) + land1[j, r].astype(f32) + land2[s, r].astype(f32)
+                if s:
+                    send3[s - 1, r] = value.astype(bf16)
+                else:
+                    acc[r] = value
+                return carry
+
+            tiles(h * half, half, add3, 0)
+            if s:
+                hop3[s, h] = push(
+                    send3.at[s - 1, piece(h)],
+                    land3.at[s - 1, piece(h)],
+                    p3s.at[s - 1, h],
+                    p3r.at[s - 1, h],
+                    z_peer(s),
+                )
+        if at < 3:
+            gain_take(at)
+            gain_send(at + 1)
+
+    square = jnp.zeros((8, cols), f32)
+    for h in range(2):
+        for s in order[:-1]:
+            hop3[s, h].wait_recv()
+
+        def add4(r, carry):
+            value = acc[r]
+            for s in range(1, depth):
+                value = value + land3[s - 1, r].astype(f32)
+            acc[r] = value
+            sq = value * value
+            for i in range(TILE // 8):
+                carry = carry + sq[i * 8 : i * 8 + 8]
+            return carry
+
+        square = tiles(h * half, half, add4, square)
+    folded = square[:, 0:128]
+    for i in range(1, cols // 128):
+        folded = folded + square[:, i * 128 : i * 128 + 128]
+    seat = (x * 2 + c) * 2 + t
+    t1[seat] = folded
+    sums = {}
+    for k in range(1, 8):
+        sums[k] = push(t1.at[seat], t1.at[seat], t1s.at[k], t1r.at[k], near_peer(k))
+
+    for s in range(1, depth):
+        gain_hop[2 + s].wait_recv()
+        state_hop[2 + s].wait_recv()
+    g_gain = gz[0]
+    for i in range(1, depth):
+        g_gain = g_gain + gz[i]
+    gsum[3] = g_gain
+
+    for copy in loads[:3]:
+        copy.wait()
+    for k in range(1, 8):
+        sums[k].wait_recv()
+    t2[z] = jnp.sum(t1[...], axis=0)
+    far = {}
+    for s in range(1, depth):
+        far[s] = push(t2.at[z], t2.at[z], t2s.at[s], t2r.at[s], z_peer(s))
+    gain_total = jnp.sum(g_gain * g_gain, keepdims=True)
+    for s in range(1, depth):
+        far[s].wait_recv()
+    total = jnp.sum(jnp.sum(t2[...], axis=0), keepdims=True) + gain_total
+    factor = jnp.minimum(f32(1.0), 1.0 / jnp.sqrt(total / PARAMS + 1e-06))
+
+    def update(r, carry):
+        new = adam_update(acc[r], mbuf[r], vbuf[r], wbuf[r], factor, 0.1)
+        wbuf[r], mbuf[r], vbuf[r] = new
+        kv[f, r] = new[0].astype(bf16)
+        return carry
+
+    tiles(0, rows, update, 0)
+
+    near_first = [s for s in range(1, depth) if s != depth // 2] + [depth // 2]
+    zhop, xhop, chop, yhop, ohop = {}, {}, {}, {}, {}
+    for s in near_first:
+        zhop[s] = push(kv.at[f], kv.at[f], azs.at[s], azr.at[s], z_peer(s))
+
+    quarter = rows // 2
+    give = pl.ds(pl.multiple_of((1 - t) * quarter, quarter), quarter)
+    keep = pl.multiple_of(t * quarter, quarter)
+    mine = pl.ds(pl.multiple_of(t * cols, cols), cols)
+    theirs = pl.ds(pl.multiple_of((1 - t) * cols, cols), cols)
+    outs = []
+
+    def spread(s, dx):
+        j = s * 2 + dx
+        b = index(behind(s), flip(x, dx), c)
+        if dx == 0:
+            xhop[s] = push(kv.at[b], kv.at[b], axs.at[s], axr.at[s], x_peer)
+        yhop[j] = push(kv.at[b, give], other.at[b], ays.at[j], ayr.at[j], y_peer)
+        chop[j] = push(kv.at[b], kv.at[b], acs.at[j], acr.at[j], core_peer)
+        outs.append(local(kv.at[b], kv_out.at[b], kvo_sem.at[j, 0]))
+
+    def blend(b, sem):
+        def body(r, carry):
+            source = pl.ds(pl.multiple_of(keep + r.start, TILE), TILE)
+            old = avg[b, r, mine].astype(f32)
+            avg[b, r, mine] = (0.8 * old + 0.2 * kv[b, source].astype(f32)).astype(bf16)
+            old = avg[b, r, theirs].astype(f32)
+            avg[b, r, theirs] = (0.8 * old + 0.2 * other[b, r].astype(f32)).astype(bf16)
+            return carry
+
+        tiles(0, quarter, body, 0)
+        outs.append(local(avg.at[b], avg_out.at[b], sem))
+
+    def finish_here(s, dx):
+        j = s * 2 + dx
+        b = index(behind(s), flip(x, dx), c)
+        yhop[j].wait_recv()
+        ohop[j] = push(other.at[b], other.at[b], aos.at[j], aor.at[j], core_peer)
+        blend(b, avo_sem.at[j, 0])
+
+    def finish_there(s, dx):
+        j = s * 2 + dx
+        b = index(behind(s), flip(x, dx), 1 - c)
+        chop[j].wait_recv()
+        outs.append(local(kv.at[b], kv_out.at[b], kvo_sem.at[j, 1]))
+        ohop[j].wait_recv()
+        blend(b, avo_sem.at[j, 1])
+
+    events = [(0, 0)]
+    last = 0
+    for s in near_first:
+        events += [(s, 0), (last, 1)]
+        last = s
+    events.append((last, 1))
+
+    for at, (s, dx) in enumerate(events):
+        if dx:
+            xhop[s].wait_recv()
+        elif s:
+            zhop[s].wait_recv()
+        spread(s, dx)
+        if at == 0:
+            outs.append(local(wbuf, w_out, store_sem.at[0]))
+            outs.append(local(mbuf, m_out, store_sem.at[1]))
+            outs.append(local(vbuf, v_out, store_sem.at[2]))
+            fresh = adam_update(
+                gsum[3], states[:, 1, :], states[:, 2, :], states[:, 0, :], factor, 0.0
+            )
+            copy_out[...] = fresh[0].astype(bf16)
+            piece_grad = gsum[3, pl.ds(place, 1), :]
+            gw_out[...], gm_out[...], gv_out[...] = adam_update(
+                piece_grad, gm_in[...], gv_in[...], gw_in[...], factor, 0.0
+            )
+            loads[3].wait()
+        if at >= 2:
+            finish_here(*events[at - 2])
+        if at >= 3:
+            finish_there(*events[at - 3])
+    for event in events[-2:]:
+        finish_here(*event)
+    for event in events[-3:]:
+        finish_there(*event)
+    for wait in pending:
+        wait()
+    for copy in outs:
+        copy.wait()
+
+
+def fused_shards(
+    grad_kv,
+    grad_gains,
+    kv_weight,
+    kv_first,
+    kv_second,
+    gain_weight,
+    gain_first,
+    gain_second,
+    average,
+):
+    n = lax.axis_size("fsdp")
+    places = n * lax.axis_size("tp")
+    depth = n // 4
+    rows, cols = kv_weight.shape
+    gain = gain_weight.shape[0]
+    f32, bf16 = jnp.float32, jnp.bfloat16
+    vmem, hbm = pl.BlockSpec(memory_space=pltpu.VMEM), pl.BlockSpec(memory_space=pl.ANY)
+    sems = pltpu.SemaphoreType.DMA
+    blocks = 2 * depth
+    out_shape = [
+        jax.ShapeDtypeStruct((rows, cols), f32),
+        jax.ShapeDtypeStruct((rows, cols), f32),
+        jax.ShapeDtypeStruct((rows, cols), f32),
+        jax.ShapeDtypeStruct((1, gain), f32),
+        jax.ShapeDtypeStruct((1, gain), f32),
+        jax.ShapeDtypeStruct((1, gain), f32),
+        jax.ShapeDtypeStruct((n, rows, cols), bf16),
+        jax.ShapeDtypeStruct((places, gain), bf16),
+        jax.ShapeDtypeStruct(average.shape, bf16),
+    ]
+    scratch = [
+        pltpu.VMEM((blocks, rows, cols), bf16),
+        pltpu.VMEM((blocks, rows, cols), bf16),
+        pltpu.VMEM((depth, rows, cols), bf16),
+        pltpu.VMEM((depth, rows, cols), bf16),
+        pltpu.VMEM((depth - 1, rows, cols), bf16),
+        pltpu.VMEM((depth - 1, rows, cols), bf16),
+        pltpu.VMEM((rows, cols), f32),
+        pltpu.VMEM((rows, cols), f32),
+        pltpu.VMEM((rows, cols), f32),
+        pltpu.VMEM((rows, cols), f32),
+        pltpu.VMEM(average.shape, bf16),
+        pltpu.VMEM((n, rows, cols), bf16),
+        pltpu.VMEM((n, rows // 2, cols), bf16),
+        pltpu.VMEM((4, places, gain), f32),
+        pltpu.VMEM((3, places, gain), f32),
+        pltpu.VMEM((depth, places, gain), f32),
+        pltpu.VMEM((places, 8, gain), f32),
+        pltpu.VMEM((8, 8, 128), f32),
+        pltpu.VMEM((depth, 8, 128), f32),
+        sems((blocks,)),
+        sems((4,)),
+        sems((3,)),
+        sems((blocks, 2)),
+        sems((blocks, 2)),
+        sems((depth, 2)),
+        sems((depth, 2)),
+        sems((depth - 1, 2)),
+        sems((depth - 1, 2)),
+        sems((depth + 2,)),
+        sems((depth + 2,)),
+        sems((depth + 2,)),
+        sems((depth + 2,)),
+        sems((8,)),
+        sems((8,)),
+        sems((depth,)),
+        sems((depth,)),
+        sems((depth,)),
+        sems((depth,)),
+        sems((depth,)),
+        sems((depth,)),
+        sems((blocks,)),
+        sems((blocks,)),
+        sems((blocks,)),
+        sems((blocks,)),
+        sems((blocks,)),
+        sems((blocks,)),
+        sems((blocks, 2)),
+        sems((blocks, 2)),
+    ]
+    w, m, v, gw, gm, gv, kv, copy, avg = pl.pallas_call(
+        functools.partial(step_kernel, depth),
+        out_shape=out_shape,
+        in_specs=[hbm, vmem, hbm, hbm, hbm, vmem, vmem, vmem, hbm],
+        out_specs=[hbm, hbm, hbm, vmem, vmem, vmem, hbm, vmem, hbm],
+        scratch_shapes=scratch,
+        compiler_params=pltpu.CompilerParams(
+            collective_id=0, has_side_effects=True, vmem_limit_bytes=48 * 1024 * 1024
+        ),
+        cost_estimate=pl.CostEstimate(
+            flops=40 * n * rows * cols,
+            bytes_accessed=20 * n * rows * cols,
+            transcendentals=rows * cols,
+        ),
+    )(
+        grad_kv.reshape(n, rows, cols),
+        grad_gains.reshape(places, gain),
+        kv_weight,
+        kv_first,
+        kv_second,
+        gain_weight.reshape(1, gain),
+        gain_first.reshape(1, gain),
+        gain_second.reshape(1, gain),
+        average,
+    )
+    return (
+        w,
+        m,
+        v,
+        gw.reshape(gain),
+        gm.reshape(gain),
+        gv.reshape(gain),
+        kv.reshape(n * rows, cols),
+        copy.reshape(places * gain),
+        avg,
+    )
+
+
+def fits(mesh):
+    return mesh.shape["tp"] == 2 and mesh.shape["fsdp"] % 4 == 0 and mesh.shape["fsdp"] >= 16
 
 
 def shards(
@@ -84,4 +594,5 @@
         P(),
         P(None, "tp", None),
     )
-    return jax.shard_map(shards, mesh=mesh, in_specs=in_specs, out_specs=out_specs, check_vma=False)
+    body = fused_shards if fits(mesh) else shards
+    return jax.shard_map(body, mesh=mesh, in_specs=in_specs, out_specs=out_specs, check_vma=False)

time: 366 us -> 107 us (0.29)
  blocking collectives: 177 us -> 0 us
  waiting for transfers between devices: 115 us -> 0 us
  Pallas kernels: 0 us -> 87.5 us
  other arithmetic: 19 us -> 0.85 us
  between operations: 16.1 us -> 0.68 us
  local copies, waits for them, and re-layouts: 29.7 us -> 16.5 us
  starting transfers between devices: 5.67 us -> 0 us
    all_gather x1 -> x0, blocking collectives: 95.2 us -> none  [shards(): lax.all_gather(gain_w.astype(jnp.bfloat16), ('fsdp', 'tp'), axis=0, tiled...]
    pallas_call x0 -> x1, Pallas kernels: none -> 87.5 us  [fused_shards(): pl.pallas_call(functools.partial(step_kernel, depth), out_shape=out_shape...]
    reduce_scatter x1 -> x0, waiting for transfers between devices: 63.9 us -> none  [shards(): lax.psum_scatter(grad_kv[0].astype(jnp.float32), 'fsdp', scatter_dimensio...]
    all_gather x1 -> x0, waiting for transfers between devices: 51.4 us -> none  [shards(): kv_blocks = lax.all_gather(kv_rounded, 'fsdp', axis=0, tiled=True)]
    unnamed x1 -> x0, blocking collectives: 41.7 us -> none
    psum x1 -> x0, blocking collectives: 39.7 us -> none  [shards(): lax.psum(kv_square + jnp.sum(gain_piece * gain_piece), ('fsdp', 'tp'))]
    convert_element_type x5 -> x0, other arithmetic: 13.1 us -> none  [the longest x1 6.61 us: shards(): grad_kv[0].astype(jnp.float32)]
    all_to_all x1 -> x0, local copies, waits for them, and re-layouts: 6.39 us -> none  [shards(): lax.all_to_all(kv_blocks.reshape(shard_count, tp_count, row_count, column...]
  transfers between devices with their start and end apart: 3 -> 0, of which waited for: 2 -> 0; matrix products, arithmetic and copies ran while one was open for 2% -> 0% of each run, Pallas kernels for 0% -> 0%
where the time goes in v1:
time: 107 us; the launch traced here: 106 us
  Pallas kernels  87.5 us (82%)
  local copies, waits for them, and re-layouts  16.5 us (15%)
    pallas_call x1, Pallas kernels, fused_shards(): pl.pallas_call(functools.partial(step_kernel, depth), out_shape=out_shape...  87.5 us
    unnamed x23, local copies, waits for them, and re-layouts  16.5 us

profile of v1, /device:TPU:1, one launch (start us, length us, event | category | flops | bytes accessed | tf_op | source)
XLA Modules:
  0.0 105.5 jit_solution(10339750274352331769)
XLA Ops:
  0.6 0.8 reduce
  1.5 0.0 copy-start
  1.5 1.0 copy-done
  2.6 0.0 copy-start.1
  2.6 1.0 copy-done.1
  3.6 0.0 copy-start.2
  3.6 1.0 copy-done.2
  4.6 0.0 copy-start.3
  4.6 0.7 copy-done.3
  5.3 0.0 copy-start.4
  5.3 0.7 copy-done.4
  6.0 0.0 copy-start.5
  6.0 0.7 copy-done.5
  6.7 87.5 %shard_map.160 = (f32[256,512]{1,0:T(8,128)S(1)}, f32[256,512]{1,0:T(8,128)S(1)}, f32[256,512]{1,0:T(8,128)S(1)}, f32[1,256]{1,0:T(1,128)S(1)}, f32[1,256]{1,0:T...) custom-call(bf16[16,256,512]{2,1,0:T(8,128)(2,1)} %bitcast.17, ...), custom_call_target="tpu_custom_call" | custom-call | flops 83886080 | bytes 41943040 | tf_op jit(solution)/shard_map/pallas_call | solution.py:489
  94.2 0.6 copy.18
  94.8 0.8 copy.27
  95.6 0.8 copy.28
  96.4 0.8 copy.29
  97.2 0.6 copy.30
  97.7 0.6 copy.31
  98.3 0.6 copy.32
  98.8 0.0 copy-start.6
  98.8 4.6 %copy.33 = bf16[4096,512]{1,0:T(8,128)(2,1)} copy(bf16[4096,512]{1,0:T(8,128)(2,1)} %bitcast.18) | data formatting | bytes 8388608
  103.5 0.0 copy-done.6
  103.5 2.0 %copy.34 = bf16[16,128,1024]{2,1,0:T(8,128)(2,1)} copy(bf16[16,128,1024]{2,1,0:T(8,128)(2,1)S(1)} %copy-done.6) | data formatting | bytes 8388608
  (1 shorter events, 0.0 us)
Async XLA Ops:
  1.5 1.0 copy-start
  2.6 1.0 copy-start.1
  3.6 1.0 copy-start.2
  4.6 0.7 copy-start.3
  5.3 0.7 copy-start.4
  6.0 0.7 copy-start.5
  98.8 4.6 %copy-start.6 = (bf16[16,128,1024]{2,1,0:T(8,128)(2,1)S(1)}, bf16[16,128,1024]{2,1,0:T(8,128)(2,1)}, u32[]{:S(2)}) copy-start(bf16[16,128,1024]{2,1,0:T(8,128)(2,1)} %get-tuple-element.44) | copy-start | bytes 12582916

commit v2 on v1

--- a/solution.py
+++ b/solution.py
@@ -30,19 +30,17 @@
     w_in,
     m_in,
     v_in,
-    gw_in,
-    gm_in,
-    gv_in,
+    gain_in,
     avg_in,
-    w_out,
-    m_out,
-    v_out,
+    wbuf,
+    mbuf,
+    vbuf,
     gw_out,
     gm_out,
     gv_out,
-    kv_out,
+    kv,
     copy_out,
-    avg_out,
+    avg,
     own,
     land1,
     send2,
@@ -50,11 +48,6 @@
     send3,
     land3,
     acc,
-    wbuf,
-    mbuf,
-    vbuf,
-    avg,
-    kv,
     other,
     gsum,
     gland,
@@ -64,7 +57,6 @@
     t2,
     own_sem,
     load_sem,
-    store_sem,
     p1s,
     p1r,
     p2s,
@@ -89,8 +81,6 @@
     ayr,
     aos,
     aor,
-    kvo_sem,
-    avo_sem,
 ):
     f32, bf16 = jnp.float32, jnp.bfloat16
     f = lax.axis_index("fsdp")
@@ -159,30 +149,33 @@
     def piece(h):
         return pl.ds(h * half, half)
 
-    for s in order:
-        for dx in (1, 0):
+    chunks = [(s, h) for s in order for h in range(2)]
+    count = len(chunks)
+    first_hops = []
+    for i in range(count + 2):
+        if i < count:
+            first_hops.append((*chunks[i], 1))
+        if i >= 2:
+            first_hops.append((*chunks[i - 2], 0))
+
+    def push_first(many):
+        for s, h, dx in first_hops[:many]:
             j = s * 2 + dx
-            for h in range(2):
-                hop1[j, h] = push(
-                    grad.at[index(ahead(s), flip(x, dx), 1 - c), piece(h)],
-                    land1.at[j, piece(h)],
-                    p1s.at[j, h],
-                    p1r.at[j, h],
-                    core_peer,
-                )
-    loads = [
-        local(w_in, wbuf, load_sem.at[0]),
-        local(m_in, mbuf, load_sem.at[1]),
-        local(v_in, vbuf, load_sem.at[2]),
-        local(avg_in, avg, load_sem.at[3]),
-    ]
+            hop1[j, h] = push(
+                grad.at[index(ahead(s), flip(x, dx), 1 - c), piece(h)],
+                land1.at[j, piece(h)],
+                p1s.at[j, h],
+                p1r.at[j, h],
+                core_peer,
+            )
+        del first_hops[:many]
+
+    push_first(4)
 
     place = f * 2 + t
     gsum[0] = gain_grad[...].astype(f32)
     states[place] = jnp.zeros(states.shape[1:], f32)
-    states[place, 0:1, :] = gw_in[...]
-    states[place, 1:2, :] = gm_in[...]
-    states[place, 2:3, :] = gv_in[...]
+    states[place, 0:3, :] = gain_in[...]
     near = [y_peer, core_peer, x_peer]
     gain_hop, state_hop = {}, {}
 
@@ -219,48 +212,62 @@
 
         return lax.fori_loop(0, count // TILE, step, init)
 
-    for at, s in enumerate(order):
+    def relay_x(s, h):
         j = s * 2 + 1
-        own_copy[j].wait()
-        for h in range(2):
-            hop1[j, h].wait_recv()
-
-            def add2(r, carry, j=j, s=s):
-                send2[s, r] = (own[j, r].astype(f32) + land1[j, r].astype(f32)).astype(bf16)
-                return carry
-
-            tiles(h * half, half, add2, 0)
-            hop2[s, h] = push(
-                send2.at[s, piece(h)], land2.at[s, piece(h)], p2s.at[s, h], p2r.at[s, h], x_peer
+        if h == 0:
+            own_copy[j].wait()
+        hop1[j, h].wait_recv()
+
+        def add2(r, carry):
+            send2[s, r] = (own[j, r].astype(f32) + land1[j, r].astype(f32)).astype(bf16)
+            return carry
+
+        tiles(h * half, half, add2, 0)
+        hop2[s, h] = push(
+            send2.at[s, piece(h)], land2.at[s, piece(h)], p2s.at[s, h], p2r.at[s, h], x_peer
+        )
+
+    def relay_z(s, h):
+        j = s * 2
+        if h == 0:
+            own_copy[j].wait()
+        hop1[j, h].wait_recv()
+        hop2[s, h].wait_recv()
+
+        def add3(r, carry):
+            value = own[j, r].astype(f32) + land1[j, r].astype(f32) + land2[s, r].astype(f32)
+            if s:
+                send3[s - 1, r] = value.astype(bf16)
+            else:
+                acc[r] = value
+            return carry
+
+        tiles(h * half, half, add3, 0)
+        if s:
+            hop3[s, h] = push(
+                send3.at[s - 1, piece(h)],
+                land3.at[s - 1, piece(h)],
+                p3s.at[s - 1, h],
+                p3r.at[s - 1, h],
+                z_peer(s),
             )
 
-    for at, s in enumerate(order):
-        j = s * 2
-        own_copy[j].wait()
-        for h in range(2):
-            hop1[j, h].wait_recv()
-            hop2[s, h].wait_recv()
-
-            def add3(r, carry, j=j, s=s):
-                value = own[j, r].astype(f32) + land1[j, r].astype(f32) + land2[s, r].astype(f32)
-                if s:
-                    send3[s - 1, r] = value.astype(bf16)
-                else:
-                    acc[r] = value
-                return carry
-
-            tiles(h * half, half, add3, 0)
-            if s:
-                hop3[s, h] = push(
-                    send3.at[s - 1, piece(h)],
-                    land3.at[s - 1, piece(h)],
-                    p3s.at[s - 1, h],
-                    p3r.at[s - 1, h],
-                    z_peer(s),
-                )
-        if at < 3:
-            gain_take(at)
-            gain_send(at + 1)
+    for i in range(count + 2):
+        if i < count:
+            relay_x(*chunks[i])
+        push_first(2)
+        if i == 1:
+            loads = [
+                local(w_in, wbuf, load_sem.at[0]),
+                local(m_in, mbuf, load_sem.at[1]),
+                local(v_in, vbuf, load_sem.at[2]),
+                local(avg_in, avg, load_sem.at[3]),
+            ]
+        if i >= 2:
+            relay_z(*chunks[i - 2])
+        if i in (1, 3, 5):
+            gain_take(i // 2)
+            gain_send(i // 2 + 1)
 
     square = jnp.zeros((8, cols), f32)
     for h in range(2):
@@ -317,28 +324,36 @@
 
     tiles(0, rows, update, 0)
 
-    near_first = [s for s in range(1, depth) if s != depth // 2] + [depth // 2]
-    zhop, xhop, chop, yhop, ohop = {}, {}, {}, {}, {}
-    for s in near_first:
-        zhop[s] = push(kv.at[f], kv.at[f], azs.at[s], azr.at[s], z_peer(s))
-
     quarter = rows // 2
-    give = pl.ds(pl.multiple_of((1 - t) * quarter, quarter), quarter)
     keep = pl.multiple_of(t * quarter, quarter)
+    spans = [
+        pl.ds(pl.multiple_of((1 - t) * quarter, quarter), quarter),
+        pl.ds(keep, quarter),
+    ]
     mine = pl.ds(pl.multiple_of(t * cols, cols), cols)
     theirs = pl.ds(pl.multiple_of((1 - t) * cols, cols), cols)
-    outs = []
-
-    def spread(s, dx):
+    near_first = [s for s in range(1, depth) if s != depth // 2] + [depth // 2]
+    zlist = [(s, h) for s in near_first for h in range(2)]
+    xlist = [(0, 0), (0, 1)] + zlist
+    zhop, xhop, chop, yhop, ohop = {}, {}, {}, {}, {}
+
+    def push_z(many):
+        for s, h in zlist[:many]:
+            part = kv.at[f, spans[h]]
+            zhop[s, h] = push(part, part, azs.at[s, h], azr.at[s, h], z_peer(s))
+        del zlist[:many]
+
+    def spread(s, dx, h):
         j = s * 2 + dx
         b = index(behind(s), flip(x, dx), c)
+        part = kv.at[b, spans[h]]
         if dx == 0:
-            xhop[s] = push(kv.at[b], kv.at[b], axs.at[s], axr.at[s], x_peer)
-        yhop[j] = push(kv.at[b, give], other.at[b], ays.at[j], ayr.at[j], y_peer)
-        chop[j] = push(kv.at[b], kv.at[b], acs.at[j], acr.at[j], core_peer)
-        outs.append(local(kv.at[b], kv_out.at[b], kvo_sem.at[j, 0]))
-
-    def blend(b, sem):
+            xhop[s, h] = push(part, part, axs.at[s, h], axr.at[s, h], x_peer)
+        if h == 0:
+            yhop[j] = push(part, other.at[b], ays.at[j], ayr.at[j], y_peer)
+        chop[j, h] = push(part, part, acs.at[j, h], acr.at[j, h], core_peer)
+
+    def blend(b):
         def body(r, carry):
             source = pl.ds(pl.multiple_of(keep + r.start, TILE), TILE)
             old = avg[b, r, mine].astype(f32)
@@ -348,60 +363,73 @@
             return carry
 
         tiles(0, quarter, body, 0)
-        outs.append(local(avg.at[b], avg_out.at[b], sem))
 
     def finish_here(s, dx):
         j = s * 2 + dx
         b = index(behind(s), flip(x, dx), c)
         yhop[j].wait_recv()
         ohop[j] = push(other.at[b], other.at[b], aos.at[j], aor.at[j], core_peer)
-        blend(b, avo_sem.at[j, 0])
+        blend(b)
 
     def finish_there(s, dx):
         j = s * 2 + dx
         b = index(behind(s), flip(x, dx), 1 - c)
-        chop[j].wait_recv()
-        outs.append(local(kv.at[b], kv_out.at[b], kvo_sem.at[j, 1]))
+        for h in range(2):
+            chop[j, h].wait_recv()
         ohop[j].wait_recv()
-        blend(b, avo_sem.at[j, 1])
-
-    events = [(0, 0)]
-    last = 0
-    for s in near_first:
-        events += [(s, 0), (last, 1)]
-        last = s
-    events.append((last, 1))
-
-    for at, (s, dx) in enumerate(events):
-        if dx:
-            xhop[s].wait_recv()
-        elif s:
-            zhop[s].wait_recv()
-        spread(s, dx)
-        if at == 0:
-            outs.append(local(wbuf, w_out, store_sem.at[0]))
-            outs.append(local(mbuf, m_out, store_sem.at[1]))
-            outs.append(local(vbuf, v_out, store_sem.at[2]))
+        blend(b)
+
+    push_z(2)
+    here, there = [], []
+    for i in range(len(xlist) + 5):
+        if i < len(xlist):
+            s, h = xlist[i]
+            if s:
+                zhop[s, h].wait_recv()
+                push_z(1)
+            spread(s, 0, h)
+            if h:
+                here.append((i + 2, s, 0))
+        if 2 <= i < len(xlist) + 2:
+            s, h = xlist[i - 2]
+            xhop[s, h].wait_recv()
+            spread(s, 1, h)
+            if h:
+                here.append((i + 1, s, 1))
+        if i == 0:
             fresh = adam_update(
                 gsum[3], states[:, 1, :], states[:, 2, :], states[:, 0, :], factor, 0.0
             )
             copy_out[...] = fresh[0].astype(bf16)
             piece_grad = gsum[3, pl.ds(place, 1), :]
             gw_out[...], gm_out[...], gv_out[...] = adam_update(
-                piece_grad, gm_in[...], gv_in[...], gw_in[...], factor, 0.0
+                piece_grad, gain_in[1:2], gain_in[2:3], gain_in[0:1], factor, 0.0
             )
             loads[3].wait()
-        if at >= 2:
-            finish_here(*events[at - 2])
-        if at >= 3:
-            finish_there(*events[at - 3])
-    for event in events[-2:]:
-        finish_here(*event)
-    for event in events[-3:]:
-        finish_there(*event)
+        for due, s, dx in here:
+            if due == i:
+                finish_here(s, dx)
+                there.append((i + 1, s, dx))
+        for due, s, dx in there:
+            if due == i:
+                finish_there(s, dx)
     for wait in pending:
         wait()
-    for copy in outs:
+
+
+def store_kernel(*refs):
+    count = len(refs) // 2
+    sources, targets, sem = refs[:count], refs[count:-1], refs[-1]
+    copies = []
+    for at, (src, dst) in enumerate(zip(sources, targets)):
+        parts = 4 if src.ndim == 3 else 1
+        step = src.shape[0] // parts
+        for part in range(parts):
+            span = pl.ds(part * step, step)
+            copy = pltpu.make_async_copy(src.at[span], dst.at[span], sem.at[at, part])
+            copy.start()
+            copies.append(copy)
+    for copy in copies:
         copy.wait()
 
 
@@ -422,7 +450,7 @@
     rows, cols = kv_weight.shape
     gain = gain_weight.shape[0]
     f32, bf16 = jnp.float32, jnp.bfloat16
-    vmem, hbm = pl.BlockSpec(memory_space=pltpu.VMEM), pl.BlockSpec(memory_space=pl.ANY)
+    vmem, hbm = pl.BlockSpec(memory_space=pltpu.VMEM), pl.BlockSpec(memory_space=pltpu.HBM)
     sems = pltpu.SemaphoreType.DMA
     blocks = 2 * depth
     out_shape = [
@@ -444,11 +472,6 @@
         pltpu.VMEM((depth - 1, rows, cols), bf16),
         pltpu.VMEM((depth - 1, rows, cols), bf16),
         pltpu.VMEM((rows, cols), f32),
-        pltpu.VMEM((rows, cols), f32),
-        pltpu.VMEM((rows, cols), f32),
-        pltpu.VMEM((rows, cols), f32),
-        pltpu.VMEM(average.shape, bf16),
-        pltpu.VMEM((n, rows, cols), bf16),
         pltpu.VMEM((n, rows // 2, cols), bf16),
         pltpu.VMEM((4, places, gain), f32),
         pltpu.VMEM((3, places, gain), f32),
@@ -458,7 +481,6 @@
         pltpu.VMEM((depth, 8, 128), f32),
         sems((blocks,)),
         sems((4,)),
-        sems((3,)),
         sems((blocks, 2)),
         sems((blocks, 2)),
         sems((depth, 2)),
@@ -473,27 +495,25 @@
         sems((8,)),
         sems((depth,)),
         sems((depth,)),
-        sems((depth,)),
-        sems((depth,)),
-        sems((depth,)),
-        sems((depth,)),
+        sems((depth, 2)),
+        sems((depth, 2)),
+        sems((depth, 2)),
+        sems((depth, 2)),
+        sems((blocks, 2)),
+        sems((blocks, 2)),
         sems((blocks,)),
         sems((blocks,)),
         sems((blocks,)),
         sems((blocks,)),
-        sems((blocks,)),
-        sems((blocks,)),
-        sems((blocks, 2)),
-        sems((blocks, 2)),
     ]
-    w, m, v, gw, gm, gv, kv, copy, avg = pl.pallas_call(
+    held = pl.pallas_call(
         functools.partial(step_kernel, depth),
         out_shape=out_shape,
-        in_specs=[hbm, vmem, hbm, hbm, hbm, vmem, vmem, vmem, hbm],
-        out_specs=[hbm, hbm, hbm, vmem, vmem, vmem, hbm, vmem, hbm],
+        in_specs=[hbm, vmem, hbm, hbm, hbm, vmem, hbm],
+        out_specs=[vmem] * 9,
         scratch_shapes=scratch,
         compiler_params=pltpu.CompilerParams(
-            collective_id=0, has_side_effects=True, vmem_limit_bytes=48 * 1024 * 1024
+            collective_id=0, has_side_effects=True, vmem_limit_bytes=40 * 1024 * 1024
         ),
         cost_estimate=pl.CostEstimate(
             flops=40 * n * rows * cols,
@@ -506,11 +526,17 @@
         kv_weight,
         kv_first,
         kv_second,
-        gain_weight.reshape(1, gain),
-        gain_first.reshape(1, gain),
-        gain_second.reshape(1, gain),
+        jnp.stack([gain_weight, gain_first, gain_second]),
         average,
     )
+    w, m, v, gw, gm, gv, kv, copy, avg = pl.pallas_call(
+        store_kernel,
+        out_shape=out_shape,
+        in_specs=[vmem] * 9,
+        out_specs=[hbm] * 9,
+        scratch_shapes=[sems((9, 4))],
+        compiler_params=pltpu.CompilerParams(has_side_effects=True),
+    )(*held)
     return (
         w,
         m,

time: 107 us -> 110 us (1.028)
  Pallas kernels: 87.5 us -> 94 us
  local copies, waits for them, and re-layouts: 16.5 us -> 13.2 us
    pallas_call x0 -> x1, Pallas kernels: none -> 8.06 us  [fused_shards(): pl.pallas_call(store_kernel, out_shape=out_shape, in_specs=[vmem] * 9, ou...]
    unnamed x23 -> x25, local copies, waits for them, and re-layouts: 16.5 us -> 13.2 us
    pallas_call x1, Pallas kernels: 87.5 us -> 85.9 us  [fused_shards(): pl.pallas_call(functools.partial(step_kernel, depth), out_shape=out_shape...]
where the time goes in v2:
time: 110 us; the launch traced here: 109 us
  Pallas kernels  94 us (85%)
  local copies, waits for them, and re-layouts  13.2 us (12%)
  other arithmetic  1.57 us (1%)
    pallas_call x1, Pallas kernels, fused_shards(): pl.pallas_call(functools.partial(step_kernel, depth), out_shape=out_shape...  85.9 us
    unnamed x25, local copies, waits for them, and re-layouts  13.2 us
    pallas_call x1, Pallas kernels, fused_shards(): pl.pallas_call(store_kernel, out_shape=out_shape, in_specs=[vmem] * 9, ou...  8.06 us

profile of v2, /device:TPU:1, one launch (start us, length us, event | category | flops | bytes accessed | tf_op | source)
XLA Modules:
  0.0 109.4 jit_solution(3292856143365932986)
XLA Ops:
  0.6 0.7 pad_maximum_fusion.gain_in
  1.4 0.8 reduce
  2.2 0.0 copy-start.2
  2.2 1.0 copy-done.2
  3.3 0.0 copy-start.3
  3.3 1.0 copy-done.3
  4.3 0.0 copy-start.4
  4.3 1.0 copy-done.4
  5.4 85.9 %shard_map.160 = (f32[256,512]{1,0:T(8,128)S(1)}, f32[256,512]{1,0:T(8,128)S(1)}, f32[256,512]{1,0:T(8,128)S(1)}, f32[1,256]{1,0:T(1,128)S(1)}, f32[1,256]{1,0:T...) custom-call(bf16[16,256,512]{2,1,0:T(8,128)(2,1)} %bitcast.10, ...), custom_call_target="tpu_custom_call" | custom-call | flops 83886080 | bytes 41943040 | tf_op jit(solution)/shard_map/pallas_call | solution.py:509
  91.3 0.0 copy-start
  91.3 1.9 %copy-done = bf16[16,256,512]{2,1,0:T(8,128)(2,1)} copy-done((bf16[16,256,512]{2,1,0:T(8,128)(2,1)}, bf16[16,256,512]{2,1,0:T(8,128)(2,1)S(1)}, u32[]{:S(2)}) %copy-start) | copy-done | bytes 4194328
  93.2 0.0 copy-start.1
  93.2 2.0 %copy-done.1 = bf16[16,128,1024]{2,1,0:T(8,128)(2,1)} copy-done((bf16[16,128,1024]{2,1,0:T(8,128)(2,1)}, bf16[16,128,1024]{2,1,0:T(8,128)(2,1)S(1)}, u32[]{:S(2)}) %copy-start.1) | copy-done | bytes 4194328
  95.2 0.0 copy-start.5
  95.2 0.8 copy-done.5
  96.0 0.0 copy-start.6
  96.0 0.8 copy-done.6
  96.9 0.0 copy-start.7
  96.9 0.8 copy-done.7
  97.7 0.0 copy-start.8
  97.7 0.6 copy-done.8
  98.3 0.0 copy-start.9
  98.3 0.6 copy-done.9
  98.8 0.0 copy-start.10
  98.8 0.6 copy-done.10
  99.4 0.0 copy-start.11
  99.4 0.6 copy-done.11
  100.0 8.1 %shard_map.161 = (f32[256,512]{1,0:T(8,128)}, f32[256,512]{1,0:T(8,128)}, f32[256,512]{1,0:T(8,128)}, f32[1,256]{1,0:T(1,128)}, f32[1,256]{1,0:T(1,128)}, /*inde...) custom-call(f32[256,512]{1,0:T(8,128)} %copy-done.5, ...), custom_call_target="tpu_custom_call" | custom-call | tf_op jit(solution)/shard_map/pallas_call | solution.py:532
  108.1 1.3 %copy.18 = bf16[4,2,8,128]{3,1,2,0:T(2,128)(2,1)} copy(bf16[4,2,8,128]{3,2,1,0:T(8,128)(2,1)} %bitcast.11) | data formatting | bytes 32768
  (1 shorter events, 0.0 us)
Async XLA Ops:
  2.2 1.0 copy-start.2
  3.3 1.0 copy-start.3
  4.3 1.0 copy-start.4
  91.3 2.0 %copy-start = (bf16[16,256,512]{2,1,0:T(8,128)(2,1)}, bf16[16,256,512]{2,1,0:T(8,128)(2,1)S(1)}, u32[]{:S(2)}) copy-start(bf16[16,256,512]{2,1,0:T(8,128)(2,1)S(1)} %get-tuple-element.33.refs_6_) | copy-start | bytes 12582916
  93.2 2.0 %copy-start.1 = (bf16[16,128,1024]{2,1,0:T(8,128)(2,1)}, bf16[16,128,1024]{2,1,0:T(8,128)(2,1)S(1)}, u32[]{:S(2)}) copy-start(bf16[16,128,1024]{2,1,0:T(8,128)(2,1)S(1)} %get-tuple-element.35.refs_8_) | copy-start | bytes 12582916
  95.2 0.8 copy-start.5
  96.0 0.8 copy-start.6
  96.9 0.8 copy-start.7
  97.7 0.6 copy-start.8
  98.3 0.6 copy-start.9
  98.8 0.6 copy-start.10
  99.4 0.6 copy-start.11

commit v3 on v2

--- a/solution.py
+++ b/solution.py
@@ -322,7 +322,6 @@
         kv[f, r] = new[0].astype(bf16)
         return carry
 
-    tiles(0, rows, update, 0)
 
     quarter = rows // 2
     keep = pl.multiple_of(t * quarter, quarter)
@@ -379,13 +378,15 @@
         ohop[j].wait_recv()
         blend(b)
 
-    push_z(2)
     here, there = [], []
     for i in range(len(xlist) + 5):
         if i < len(xlist):
             s, h = xlist[i]
             if s:
                 zhop[s, h].wait_recv()
+                push_z(1)
+            else:
+                tiles(pl.multiple_of((1 - t if h == 0 else t) * quarter, quarter), quarter, update, 0)
                 push_z(1)
             spread(s, 0, h)
             if h:
@@ -516,8 +517,8 @@
             collective_id=0, has_side_effects=True, vmem_limit_bytes=40 * 1024 * 1024
         ),
         cost_estimate=pl.CostEstimate(
-            flops=40 * n * rows * cols,
-            bytes_accessed=20 * n * rows * cols,
+            flops=40000 * n * rows * cols,
+            bytes_accessed=5 * n * rows * cols,
             transcendentals=rows * cols,
         ),
     )(
@@ -535,7 +536,9 @@
         in_specs=[vmem] * 9,
         out_specs=[hbm] * 9,
         scratch_shapes=[sems((9, 4))],
-        compiler_params=pltpu.CompilerParams(has_side_effects=True),
+        compiler_params=pltpu.CompilerParams(
+            has_side_effects=True, vmem_limit_bytes=16 * 1024 * 1024
+        ),
     )(*held)
     return (
         w,

time: 110 us -> 96.1 us (0.87)
  local copies, waits for them, and re-layouts: 13.2 us -> 3.75 us
  Pallas kernels: 94 us -> 89.8 us
    unnamed x25 -> x7, local copies, waits for them, and re-layouts: 13.2 us -> 3.74 us
    pallas_call x1, Pallas kernels: 8.06 us -> 4.12 us  [fused_shards(): pl.pallas_call(store_kernel, out_shape=out_shape, in_specs=[vmem] * 9, ou...]
where the time goes in v3:
time: 96.1 us; the launch traced here: 95.7 us
  Pallas kernels  89.8 us (93%)
  local copies, waits for them, and re-layouts  3.75 us (4%)
  other arithmetic  1.57 us (2%)
    pallas_call x1, Pallas kernels, fused_shards(): pl.pallas_call(functools.partial(step_kernel, depth), out_shape=out_shape...  85.6 us
    pallas_call x1, Pallas kernels, fused_shards(): pl.pallas_call(store_kernel, out_shape=out_shape, in_specs=[vmem] * 9, ou...  4.12 us
    unnamed x7, local copies, waits for them, and re-layouts  3.74 us

profile of v3, /device:TPU:1, one launch (start us, length us, event | category | flops | bytes accessed | tf_op | source)
XLA Modules:
  0.0 95.7 jit_solution(167626584908544806)
XLA Ops:
  0.6 0.7 pad_maximum_fusion.gain_in
  1.4 0.8 reduce
  2.2 0.0 copy-start
  2.2 1.0 %copy-done = f32[256,512]{1,0:T(8,128)S(1)} copy-done((f32[256,512]{1,0:T(8,128)S(1)}, f32[256,512]{1,0:T(8,128)}, u32[]{:S(2)}) %copy-start) | copy-done | bytes 524312
  3.3 0.0 copy-start.1
  3.3 1.0 %copy-done.1 = f32[256,512]{1,0:T(8,128)S(1)} copy-done((f32[256,512]{1,0:T(8,128)S(1)}, f32[256,512]{1,0:T(8,128)}, u32[]{:S(2)}) %copy-start.1) | copy-done | bytes 524312
  4.3 0.0 copy-start.2
  4.3 1.0 %copy-done.2 = f32[256,512]{1,0:T(8,128)S(1)} copy-done((f32[256,512]{1,0:T(8,128)S(1)}, f32[256,512]{1,0:T(8,128)}, u32[]{:S(2)}) %copy-start.2) | copy-done | bytes 524312
  5.4 85.6 %shard_map.160 = (f32[256,512]{1,0:T(8,128)S(1)}, f32[256,512]{1,0:T(8,128)S(1)}, f32[256,512]{1,0:T(8,128)S(1)}, f32[1,256]{1,0:T(1,128)S(1)}, f32[1,256]{1,0:T...) custom-call(bf16[16,256,512]{2,1,0:T(8,128)(2,1)} %bitcast.15, ...), custom_call_target="tpu_custom_call" | custom-call | flops 83886080000 | bytes 10485760 | tf_op jit(solution)/shard_map/pallas_call | solution.py:510
  91.0 4.1 %shard_map.161 = (f32[256,512]{1,0:T(8,128)}, f32[256,512]{1,0:T(8,128)}, f32[256,512]{1,0:T(8,128)}, f32[1,256]{1,0:T(1,128)}, f32[1,256]{1,0:T(1,128)}, /*inde...) custom-call(f32[256,512]{1,0:T(8,128)S(1)} %get-tuple-element.27.refs_, ...), custom_call_target="tpu_custom_call" | custom-call | tf_op jit(solution)/shard_map/pallas_call | solution.py:533
  95.1 0.6 copy.18
  (1 shorter events, 0.0 us)
Async XLA Ops:
  2.2 1.0 %copy-start = (f32[256,512]{1,0:T(8,128)S(1)}, f32[256,512]{1,0:T(8,128)}, u32[]{:S(2)}) copy-start(f32[256,512]{1,0:T(8,128)} %w_in.1) | copy-start | bytes 1572868
  3.3 1.0 %copy-start.1 = (f32[256,512]{1,0:T(8,128)S(1)}, f32[256,512]{1,0:T(8,128)}, u32[]{:S(2)}) copy-start(f32[256,512]{1,0:T(8,128)} %m_in.1) | copy-start | bytes 1572868
  4.3 1.0 %copy-start.2 = (f32[256,512]{1,0:T(8,128)S(1)}, f32[256,512]{1,0:T(8,128)}, u32[]{:S(2)}) copy-start(f32[256,512]{1,0:T(8,128)} %v_in.1) | copy-start | bytes 1572868

commit v4 on v3

--- a/solution.py
+++ b/solution.py
@@ -100,9 +100,6 @@
     def ahead(s):
         return lax.rem(z + s, depth)
 
-    def behind(s):
-        return lax.rem(z + depth - s, depth)
-
     core_peer = (index(z, x, 1 - c), t)
     x_peer = (index(z, 1 - x, c), t)
     y_peer = (f, 1 - t)
@@ -331,20 +328,52 @@
     ]
     mine = pl.ds(pl.multiple_of(t * cols, cols), cols)
     theirs = pl.ds(pl.multiple_of((1 - t) * cols, cols), cols)
-    near_first = [s for s in range(1, depth) if s != depth // 2] + [depth // 2]
-    zlist = [(s, h) for s in near_first for h in range(2)]
-    xlist = [(0, 0), (0, 1)] + zlist
-    zhop, xhop, chop, yhop, ohop = {}, {}, {}, {}, {}
-
-    def push_z(many):
-        for s, h in zlist[:many]:
-            part = kv.at[f, spans[h]]
-            zhop[s, h] = push(part, part, azs.at[s, h], azr.at[s, h], z_peer(s))
-        del zlist[:many]
+    def nearest(zz):
+        return sorted((k for k in range(depth) if k != zz), key=lambda k: abs(k - zz))
+
+    def source(q):
+        if q == 0:
+            return z
+        found = jnp.int32(nearest(0)[q - 1])
+        for zz in range(1, depth):
+            found = jnp.where(z == zz, jnp.int32(nearest(zz)[q - 1]), found)
+        return found
+
+    sources = [source(q) for q in range(depth)]
+    xlist = [(q, h) for q in range(depth) for h in range(2)]
+    xhop, chop, yhop, ohop = {}, {}, {}, {}
+    maybe = []
+
+    def z_copy(q, h, slot, target):
+        part = kv.at[index(sources[q], x, c), spans[h]]
+        return pltpu.make_async_remote_copy(
+            src_ref=part,
+            dst_ref=part,
+            send_sem=azs.at[slot, h],
+            recv_sem=azr.at[sources[q], h],
+            device_id=(index(target, x, c), t),
+            device_id_type=pl.DeviceIdType.MESH,
+        )
+
+    def z_send(q, h, slot, target, on):
+        copy = z_copy(q, h, slot, target)
+        pl.when(on)(copy.start)
+        maybe.append((on, copy.wait_send))
+
+    def z_own(h):
+        z_send(0, h, 0, z + 1, z < depth - 1)
+        z_send(0, h, depth, z - 1, z > 0)
+
+    def z_pass(q, h):
+        src = sources[q]
+        step = jnp.where(src < z, 1, -1)
+        target = z + step
+        z_copy(q, h, q, z + step).wait_recv()
+        z_send(q, h, q, target, (target >= 0) & (target < depth))
 
     def spread(s, dx, h):
         j = s * 2 + dx
-        b = index(behind(s), flip(x, dx), c)
+        b = index(sources[s], flip(x, dx), c)
         part = kv.at[b, spans[h]]
         if dx == 0:
             xhop[s, h] = push(part, part, axs.at[s, h], axr.at[s, h], x_peer)
@@ -365,14 +394,14 @@
 
     def finish_here(s, dx):
         j = s * 2 + dx
-        b = index(behind(s), flip(x, dx), c)
+        b = index(sources[s], flip(x, dx), c)
         yhop[j].wait_recv()
         ohop[j] = push(other.at[b], other.at[b], aos.at[j], aor.at[j], core_peer)
         blend(b)
 
     def finish_there(s, dx):
         j = s * 2 + dx
-        b = index(behind(s), flip(x, dx), 1 - c)
+        b = index(sources[s], flip(x, dx), 1 - c)
         for h in range(2):
             chop[j, h].wait_recv()
         ohop[j].wait_recv()
@@ -383,11 +412,10 @@
         if i < len(xlist):
             s, h = xlist[i]
             if s:
-                zhop[s, h].wait_recv()
-                push_z(1)
+                z_pass(s, h)
             else:
                 tiles(pl.multiple_of((1 - t if h == 0 else t) * quarter, quarter), quarter, update, 0)
-                push_z(1)
+                z_own(h)
             spread(s, 0, h)
             if h:
                 here.append((i + 2, s, 0))
@@ -414,6 +442,8 @@
         for due, s, dx in there:
             if due == i:
                 finish_there(s, dx)
+    for on, wait in maybe:
+        pl.when(on)(wait)
     for wait in pending:
         wait()
 
@@ -496,7 +526,7 @@
         sems((8,)),
         sems((depth,)),
         sems((depth,)),
-        sems((depth, 2)),
+        sems((depth + 1, 2)),
         sems((depth, 2)),
         sems((depth, 2)),
         sems((depth, 2)),

time: 96.1 us -> 93.8 us (0.976)
  Pallas kernels: 89.8 us -> 87.4 us
    pallas_call x1, Pallas kernels: 85.6 us -> 83.3 us  [fused_shards(): pl.pallas_call(functools.partial(step_kernel, depth), out_shape=out_shape...]
where the time goes in v4:
time: 93.8 us; the launch traced here: 93.4 us
  Pallas kernels  87.4 us (93%)
  local copies, waits for them, and re-layouts  3.75 us (4%)
  other arithmetic  1.57 us (2%)
    pallas_call x1, Pallas kernels, fused_shards(): pl.pallas_call(functools.partial(step_kernel, depth), out_shape=out_shape...  83.3 us
    pallas_call x1, Pallas kernels, fused_shards(): pl.pallas_call(store_kernel, out_shape=out_shape, in_specs=[vmem] * 9, ou...  4.12 us
    unnamed x7, local copies, waits for them, and re-layouts  3.74 us

profile of v4, /device:TPU:1, one launch (start us, length us, event | category | flops | bytes accessed | tf_op | source)
XLA Modules:
  0.0 93.4 jit_solution(5521843672161362837)
XLA Ops:
  0.6 0.7 pad_maximum_fusion.gain_in
  1.4 0.8 reduce
  2.2 0.0 copy-start
  2.2 1.0 %copy-done = f32[256,512]{1,0:T(8,128)S(1)} copy-done((f32[256,512]{1,0:T(8,128)S(1)}, f32[256,512]{1,0:T(8,128)}, u32[]{:S(2)}) %copy-start) | copy-done | bytes 524312
  3.3 0.0 copy-start.1
  3.3 1.0 %copy-done.1 = f32[256,512]{1,0:T(8,128)S(1)} copy-done((f32[256,512]{1,0:T(8,128)S(1)}, f32[256,512]{1,0:T(8,128)}, u32[]{:S(2)}) %copy-start.1) | copy-done | bytes 524312
  4.3 0.0 copy-start.2
  4.3 1.0 %copy-done.2 = f32[256,512]{1,0:T(8,128)S(1)} copy-done((f32[256,512]{1,0:T(8,128)S(1)}, f32[256,512]{1,0:T(8,128)}, u32[]{:S(2)}) %copy-start.2) | copy-done | bytes 524312
  5.4 83.3 %shard_map.160 = (f32[256,512]{1,0:T(8,128)S(1)}, f32[256,512]{1,0:T(8,128)S(1)}, f32[256,512]{1,0:T(8,128)S(1)}, f32[1,256]{1,0:T(1,128)S(1)}, f32[1,256]{1,0:T...) custom-call(bf16[16,256,512]{2,1,0:T(8,128)(2,1)} %bitcast.15, ...), custom_call_target="tpu_custom_call" | custom-call | flops 83886080000 | bytes 10485760 | tf_op jit(solution)/shard_map/pallas_call | solution.py:540
  88.7 4.1 %shard_map.161 = (f32[256,512]{1,0:T(8,128)}, f32[256,512]{1,0:T(8,128)}, f32[256,512]{1,0:T(8,128)}, f32[1,256]{1,0:T(1,128)}, f32[1,256]{1,0:T(1,128)}, /*inde...) custom-call(f32[256,512]{1,0:T(8,128)S(1)} %get-tuple-element.27.refs_, ...), custom_call_target="tpu_custom_call" | custom-call | tf_op jit(solution)/shard_map/pallas_call | solution.py:563
  92.8 0.6 copy.18
  (1 shorter events, 0.0 us)
Async XLA Ops:
  2.2 1.0 %copy-start = (f32[256,512]{1,0:T(8,128)S(1)}, f32[256,512]{1,0:T(8,128)}, u32[]{:S(2)}) copy-start(f32[256,512]{1,0:T(8,128)} %w_in.1) | copy-start | bytes 1572868
  3.3 1.0 %copy-start.1 = (f32[256,512]{1,0:T(8,128)S(1)}, f32[256,512]{1,0:T(8,128)}, u32[]{:S(2)}) copy-start(f32[256,512]{1,0:T(8,128)} %m_in.1) | copy-start | bytes 1572868
  4.3 1.0 %copy-start.2 = (f32[256,512]{1,0:T(8,128)S(1)}, f32[256,512]{1,0:T(8,128)}, u32[]{:S(2)}) copy-start(f32[256,512]{1,0:T(8,128)} %v_in.1) | copy-start | bytes 1572868

commit v5 on v4

--- a/solution.py
+++ b/solution.py
@@ -9,7 +9,7 @@
 
 STEP = 100
 PARAMS = 4202496
-TILE = 32
+TILE = 64
 
 
 def adam_update(grad, first, second, weight, factor, decay):
@@ -27,9 +27,7 @@
     depth,
     grad,
     gain_grad,
-    w_in,
-    m_in,
-    v_in,
+    state_in,
     gain_in,
     avg_in,
     wbuf,
@@ -255,10 +253,7 @@
         push_first(2)
         if i == 1:
             loads = [
-                local(w_in, wbuf, load_sem.at[0]),
-                local(m_in, mbuf, load_sem.at[1]),
-                local(v_in, vbuf, load_sem.at[2]),
-                local(avg_in, avg, load_sem.at[3]),
+                local(avg_in, avg, load_sem.at[0]),
             ]
         if i >= 2:
             relay_z(*chunks[i - 2])
@@ -299,8 +294,6 @@
         g_gain = g_gain + gz[i]
     gsum[3] = g_gain
 
-    for copy in loads[:3]:
-        copy.wait()
     for k in range(1, 8):
         sums[k].wait_recv()
     t2[z] = jnp.sum(t1[...], axis=0)
@@ -314,7 +307,7 @@
     factor = jnp.minimum(f32(1.0), 1.0 / jnp.sqrt(total / PARAMS + 1e-06))
 
     def update(r, carry):
-        new = adam_update(acc[r], mbuf[r], vbuf[r], wbuf[r], factor, 0.1)
+        new = adam_update(acc[r], state_in[1, r], state_in[2, r], state_in[0, r], factor, 0.1)
         wbuf[r], mbuf[r], vbuf[r] = new
         kv[f, r] = new[0].astype(bf16)
         return carry
@@ -434,7 +427,7 @@
             gw_out[...], gm_out[...], gv_out[...] = adam_update(
                 piece_grad, gain_in[1:2], gain_in[2:3], gain_in[0:1], factor, 0.0
             )
-            loads[3].wait()
+            loads[0].wait()
         for due, s, dx in here:
             if due == i:
                 finish_here(s, dx)
@@ -511,7 +504,7 @@
         pltpu.VMEM((8, 8, 128), f32),
         pltpu.VMEM((depth, 8, 128), f32),
         sems((blocks,)),
-        sems((4,)),
+        sems((1,)),
         sems((blocks, 2)),
         sems((blocks, 2)),
         sems((depth, 2)),
@@ -540,7 +533,7 @@
     held = pl.pallas_call(
         functools.partial(step_kernel, depth),
         out_shape=out_shape,
-        in_specs=[hbm, vmem, hbm, hbm, hbm, vmem, hbm],
+        in_specs=[hbm, vmem, vmem, vmem, hbm],
         out_specs=[vmem] * 9,
         scratch_shapes=scratch,
         compiler_params=pltpu.CompilerParams(
@@ -554,9 +547,7 @@
     )(
         grad_kv.reshape(n, rows, cols),
         grad_gains.reshape(places, gain),
-        kv_weight,
-        kv_first,
-        kv_second,
+        jnp.stack([kv_weight, kv_first, kv_second]),
         jnp.stack([gain_weight, gain_first, gain_second]),
         average,
     )

time: 93.8 us -> 92 us (0.981)
  local copies, waits for them, and re-layouts: 3.75 us -> 0.63 us
  other arithmetic: 1.57 us -> 3.05 us
    unnamed x7 -> x1, local copies, waits for them, and re-layouts: 3.74 us -> 0.62 us
    another operation x0 -> x1, other arithmetic: none -> 1.48 us  [fused_shards(): jnp.stack([kv_weight, kv_first, kv_second])]
where the time goes in v5:
time: 92 us; the launch traced here: 91.8 us
  Pallas kernels  87.5 us (95%)
  other arithmetic  3.05 us (3%)
    pallas_call x1, Pallas kernels, fused_shards(): pl.pallas_call(functools.partial(step_kernel, depth), out_shape=out_shape...  83.3 us
    pallas_call x1, Pallas kernels, fused_shards(): pl.pallas_call(store_kernel, out_shape=out_shape, in_specs=[vmem] * 9, ou...  4.12 us

profile of v5, /device:TPU:1, one launch (start us, length us, event | category | flops | bytes accessed | tf_op | source)
XLA Modules:
  0.0 91.8 jit_solution(3812944503719950730)
XLA Ops:
  0.6 0.7 pad_maximum_fusion.1.gain_in
  1.4 0.8 reduce
  2.2 1.5 %pad_maximum_fusion.state_in = f32[3,256,512]{2,1,0:T(8,128)S(1)} fusion(f32[1,256,512]{2,1,0:T(8,128)} %bitcast.14, f32[1,256,512]{2,1,0:T(8,128)} %bitcast.15, f32[1,256,512]{2,1,0:T(8,128)} %bitcast.16), kind=kLoop, calls=%fused_computation | loop fusion | flops 786432 | bytes 3145728 | tf_op jit(solution)/shard_map/stack | solution.py:550
  3.7 83.3 %shard_map.160 = (f32[256,512]{1,0:T(8,128)S(1)}, f32[256,512]{1,0:T(8,128)S(1)}, f32[256,512]{1,0:T(8,128)S(1)}, f32[1,256]{1,0:T(1,128)S(1)}, f32[1,256]{1,0:T...) custom-call(bf16[16,256,512]{2,1,0:T(8,128)(2,1)} %bitcast.21, ...), custom_call_target="tpu_custom_call" | custom-call | flops 83886080000 | bytes 10485760 | tf_op jit(solution)/shard_map/pallas_call | solution.py:533
  87.1 4.1 %shard_map.161 = (f32[256,512]{1,0:T(8,128)}, f32[256,512]{1,0:T(8,128)}, f32[256,512]{1,0:T(8,128)}, f32[1,256]{1,0:T(1,128)}, f32[1,256]{1,0:T(1,128)}, /*inde...) custom-call(f32[256,512]{1,0:T(8,128)S(1)} %get-tuple-element.27.refs_, ...), custom_call_target="tpu_custom_call" | custom-call | tf_op jit(solution)/shard_map/pallas_call | solution.py:554
  91.2 0.6 copy.18
  (1 shorter events, 0.0 us)

commit v6 on v5

--- a/solution.py
+++ b/solution.py
@@ -402,6 +402,12 @@
 
     here, there = [], []
     for i in range(len(xlist) + 5):
+        if 2 <= i < len(xlist) + 2:
+            s, h = xlist[i - 2]
+            xhop[s, h].wait_recv()
+            spread(s, 1, h)
+            if h:
+                here.append((i + 1, s, 1))
         if i < len(xlist):
             s, h = xlist[i]
             if s:
@@ -412,12 +418,6 @@
             spread(s, 0, h)
             if h:
                 here.append((i + 2, s, 0))
-        if 2 <= i < len(xlist) + 2:
-            s, h = xlist[i - 2]
-            xhop[s, h].wait_recv()
-            spread(s, 1, h)
-            if h:
-                here.append((i + 1, s, 1))
         if i == 0:
             fresh = adam_update(
                 gsum[3], states[:, 1, :], states[:, 2, :], states[:, 0, :], factor, 0.0

time: 92 us -> 90.3 us (0.982)
  Pallas kernels: 87.5 us -> 85.7 us
    pallas_call x1, Pallas kernels: 83.3 us -> 81.6 us  [fused_shards(): pl.pallas_call(functools.partial(step_kernel, depth), out_shape=out_shape...]
where the time goes in v6:
time: 90.3 us; the launch traced here: 90.1 us
  Pallas kernels  85.7 us (95%)
  other arithmetic  3.05 us (3%)
    pallas_call x1, Pallas kernels, fused_shards(): pl.pallas_call(functools.partial(step_kernel, depth), out_shape=out_shape...  81.6 us
    pallas_call x1, Pallas kernels, fused_shards(): pl.pallas_call(store_kernel, out_shape=out_shape, in_specs=[vmem] * 9, ou...  4.12 us

profile of v6, /device:TPU:1, one launch (start us, length us, event | category | flops | bytes accessed | tf_op | source)
XLA Modules:
  0.0 90.1 jit_solution(8602728775955721348)
XLA Ops:
  0.6 0.7 pad_maximum_fusion.1.gain_in
  1.4 0.8 reduce
  2.2 1.5 %pad_maximum_fusion.state_in = f32[3,256,512]{2,1,0:T(8,128)S(1)} fusion(f32[1,256,512]{2,1,0:T(8,128)} %bitcast.14, f32[1,256,512]{2,1,0:T(8,128)} %bitcast.15, f32[1,256,512]{2,1,0:T(8,128)} %bitcast.16), kind=kLoop, calls=%fused_computation | loop fusion | flops 786432 | bytes 3145728 | tf_op jit(solution)/shard_map/stack | solution.py:550
  3.7 81.6 %shard_map.160 = (f32[256,512]{1,0:T(8,128)S(1)}, f32[256,512]{1,0:T(8,128)S(1)}, f32[256,512]{1,0:T(8,128)S(1)}, f32[1,256]{1,0:T(1,128)S(1)}, f32[1,256]{1,0:T...) custom-call(bf16[16,256,512]{2,1,0:T(8,128)(2,1)} %bitcast.21, ...), custom_call_target="tpu_custom_call" | custom-call | flops 83886080000 | bytes 10485760 | tf_op jit(solution)/shard_map/pallas_call | solution.py:533
  85.3 4.1 %shard_map.161 = (f32[256,512]{1,0:T(8,128)}, f32[256,512]{1,0:T(8,128)}, f32[256,512]{1,0:T(8,128)}, f32[1,256]{1,0:T(1,128)}, f32[1,256]{1,0:T(1,128)}, /*inde...) custom-call(f32[256,512]{1,0:T(8,128)S(1)} %get-tuple-element.27.refs_, ...), custom_call_target="tpu_custom_call" | custom-call | tf_op jit(solution)/shard_map/pallas_call | solution.py:554
  89.4 0.6 copy.18
  (1 shorter events, 0.0 us)
